TPU v7x, 256 devices: a whole 4x4x8 slice. The times are simulated.
256 devices in a mesh: dp: 16 (over y, z_hi, core), section: 4 (over z_lo), tensor: 4 (over x).
Axes of the slice: x: 4, y: 4, z: 8 (z_hi: 2, z_lo: 4; z = z_hi * 4 + z_lo), core: 2. Of those that a mesh axis runs over, the one named last changes fastest.
Arguments:
- upstream_derivative: bfloat16 [4, 512, 8192], P(None, 'dp', 'tensor'), may hold values from -6 to 6
- stored_level_activations: bfloat16 [4, 4, 512, 8192], P('section', None, 'dp', 'tensor'), may hold values from -6 to 6
- fixed_projection_matrix: bfloat16 [4, 8192, 8192], P('section', 'tensor', 'dp'), may hold values from -0.0625 to 0.0625
- lowrank_left_matrices: bfloat16 [4, 8192, 256], P('section', 'tensor'), may hold values from -0.0625 to 0.0625
- lowrank_right_matrices: bfloat16 [4, 256, 8192], P('section', None, 'tensor'), may hold values from -0.0625 to 0.0625
- mixture_coefficients: float32 [4, 512, 64], P(None, 'dp', 'section'), may hold values from 0.05 to 1
- classifier_feature_states: bfloat16 [4, 512, 8192], P(None, 'dp', 'tensor'), may hold values from -6 to 6
- classifier_matrix: float32 [8192, 64], P('tensor', 'section'), may hold values from -0.75 to 0.75
Outputs:
- input_grads: bfloat16 [4, 4, 512, 8192], P('section', None, 'dp', 'tensor')
- scale_grads: float32 [4, 512, 64], P(None, 'dp', 'section')
- head_grad: float32 [8192, 64], P('tensor', 'section')
- hidden_grad: float32 [4, 512, 8192], P(None, 'dp', 'tensor')
All inputs are finite; a program needn't handle non-finite values.
Results may differ from a plain program's by a relative error of at most 0.008.
Values may be sent and summed in bfloat16 or wider, within the bound.
A program may use at most 128 MiB of HBM per device.

v0:
```python
import math

import jax
import jax.numpy as jnp
from jax import lax
from jax.sharding import PartitionSpec as P


def from_behind(value, axis, steps):
    count = lax.axis_size(axis)
    first, last = (max(0, -steps), min(count, count - steps))
    return lax.ppermute(value, axis, [(source, source + steps) for source in range(first, last)])


def on_device(
    upstream_derivative,
    stored_level_activations,
    fixed_projection_matrix,
    lowrank_left_matrices,
    lowrank_right_matrices,
    mixture_coefficients,
    classifier_feature_states,
    classifier_matrix,
):
    sections = lax.axis_size("section")
    position = lax.axis_index("section")
    groups = lax.axis_size("dp")
    micro = upstream_derivative.shape[0]
    rows = upstream_derivative.shape[1]
    width = upstream_derivative.shape[2]
    specialist_sequence = mixture_coefficients.shape[2]
    rank = lowrank_left_matrices.shape[2] // specialist_sequence
    block = fixed_projection_matrix[0]
    adapt_down = lowrank_left_matrices[0]
    adapt_up = lowrank_right_matrices[0]
    saved = stored_level_activations[0]
    grad_out = jnp.zeros((micro, rows, width), jnp.bfloat16)
    scale_out = jnp.zeros((micro, rows, specialist_sequence), jnp.float32)
    arriving = jnp.zeros((rows, width), jnp.bfloat16)
    ticks = micro + sections - 1
    for tick in range(ticks):
        slot = tick - (sections - 1 - position)
        valid = jnp.logical_and(slot >= 0, slot < micro)
        chosen_specialist = jnp.clip(slot, 0, micro - 1)
        from_top = lax.dynamic_index_in_dim(
            upstream_derivative, chosen_specialist, 0, keepdims=False
        )
        incoming = jnp.where(position == sections - 1, from_top, arriving)
        hidden = lax.dynamic_index_in_dim(saved, chosen_specialist, 0, keepdims=False)
        mixing_coefficient = lax.dynamic_index_in_dim(
            mixture_coefficients, chosen_specialist, 0, keepdims=False
        )
        base = None
        partial_block = jnp.dot(
            lax.all_gather(incoming, "dp", axis=0, tiled=True),
            block,
            preferred_element_type=jnp.float32,
        )
        spread = lax.all_to_all(partial_block, "dp", split_axis=0, concat_axis=1, tiled=True)
        base = lax.psum_scatter(spread, "tensor", scatter_dimension=1, tiled=True)
        down_part = jnp.dot(hidden, adapt_down, preferred_element_type=jnp.float32)
        back_part = jnp.dot(incoming, adapt_up.T, preferred_element_type=jnp.float32)
        down_full, back_full = lax.psum((down_part, back_part), "tensor")
        sgrad = (down_full * back_full).reshape(rows, specialist_sequence, rank).sum(axis=-1)
        weighted = (
            (back_full.reshape(rows, specialist_sequence, rank) * mixing_coefficient[:, :, None])
            .reshape(rows, specialist_sequence * rank)
            .astype(jnp.bfloat16)
        )
        adapter = jnp.dot(weighted, adapt_down.T, preferred_element_type=jnp.float32)
        newest = (incoming.astype(jnp.float32) + base + adapter).astype(jnp.bfloat16)
        grad_out = jnp.where(
            valid, lax.dynamic_update_index_in_dim(grad_out, newest, chosen_specialist, 0), grad_out
        )
        scale_out = jnp.where(
            valid,
            lax.dynamic_update_index_in_dim(scale_out, sgrad, chosen_specialist, 0),
            scale_out,
        )
        if tick + 1 < ticks:
            arriving = from_behind(newest, "section", -1)
    states = classifier_feature_states.reshape(-1, width).astype(jnp.float32)
    flat_scales = scale_out.reshape(-1, specialist_sequence)
    total = micro * rows * groups
    local_head = jnp.dot(states.T, flat_scales, precision=lax.Precision.HIGHEST)
    head_grad = lax.psum(local_head, "dp") * (1.0 / math.sqrt(total))
    partial_hidden = jnp.dot(flat_scales, classifier_matrix.T, precision=lax.Precision.HIGHEST)
    hidden_grad = lax.psum(partial_hidden, "section").reshape(micro, rows, width)
    return (grad_out[None], scale_out, head_grad, hidden_grad)


def solution(mesh):
    placed = (
        P(None, "dp", "tensor"),
        P("section", None, "dp", "tensor"),
        P("section", "tensor", "dp"),
        P("section", "tensor", None),
        P("section", None, "tensor"),
        P(None, "dp", "section"),
        P(None, "dp", "tensor"),
        P("tensor", "section"),
    )
    return jax.shard_map(
        on_device,
        mesh=mesh,
        in_specs=placed,
        out_specs=(
            P("section", None, "dp", "tensor"),
            P(None, "dp", "section"),
            P("tensor", "section"),
            P(None, "dp", "tensor"),
        ),
        check_vma=False,
    )
```

profile of v0, /device:TPU:1, one launch (start us, length us, event | category | flops | bytes accessed | tf_op | source)
XLA Modules:
  0.0 1237.1 jit_solution(10975911896922718510)
XLA Ops:
  9.0 69.5 %all-gather.21.cloned.1.call-done = bf16[1,512,2048]{2,1,0:T(8,128)(2,1)} async-done(((bf16[1,32,2048]{2,1,0:T(8,128)(2,1)}), bf16[1,512,2048]{2,1,0:T(8,128)(2,1)}) %all-gather.21.cloned.1.call-update) | async-done | bytes 2097168 | tf_op jit(solution)/shard_map/all_gather | solution.py:55
  81.3 23.8 %all_to_all.112 = f32[16,32,512]{2,1,0:T(8,128)S(1)} all-to-all(f32[16,32,512]{2,1,0:T(8,128)S(1)} %fusion.13), channel_id=1, replica_groups=mesh['dp'=16,'section'=4,'tensor'=4] {'dp'}, dimensions={0} | all-to-all | bytes 2097152 | tf_op jit(solution)/shard_map/all_to_all | solution.py:59
  108.6 13.2 %psum.112 = f32[32,256]{1,0:T(8,128)S(1)} all-reduce(f32[32,256]{1,0:T(8,128)S(1)} %fusion.54), channel_id=1, replica_groups=mesh['dp'=16,'section'=4,'tensor'=4] {'tensor'}, use_global_device_ids=true, to_apply=%region_1.2 | all-reduce | flops 8192 | bytes 65536 | tf_op jit(solution)/shard_map/psum | solution.py:63
  121.9 15.7 %reduce-scatter.8.cloned.1.call-done = f32[32,2048]{1,0:T(8,128)} async-done(((f32[32,8192]{1,0:T(8,128)}), f32[32,2048]{1,0:T(8,128)}) %reduce-scatter.8.cloned.1.call-update) | async-done | bytes 262160 | tf_op jit(solution)/shard_map/reduce_scatter | solution.py:60
  148.0 65.6 %all-gather.9.cloned.1.call-done = bf16[512,2048]{1,0:T(8,128)(2,1)} async-done(((bf16[32,2048]{1,0:T(8,128)(2,1)}), bf16[512,2048]{1,0:T(8,128)(2,1)}) %all-gather.9.cloned.1.call-update) | async-done | bytes 2097168 | tf_op jit(solution)/shard_map/all_gather | solution.py:55
  216.4 23.8 %all_to_all.113 = f32[16,32,512]{2,1,0:T(8,128)S(1)} all-to-all(f32[16,32,512]{2,1,0:T(8,128)S(1)} %fusion.11), channel_id=1, replica_groups=mesh['dp'=16,'section'=4,'tensor'=4] {'dp'}, dimensions={0} | all-to-all | bytes 2097152 | tf_op jit(solution)/shard_map/all_to_all | solution.py:59
  243.1 13.2 %psum.113 = f32[32,256]{1,0:T(8,128)S(1)} all-reduce(f32[32,256]{1,0:T(8,128)S(1)} %fusion.52), channel_id=1, replica_groups=mesh['dp'=16,'section'=4,'tensor'=4] {'tensor'}, use_global_device_ids=true, to_apply=%region_3.4 | all-reduce | flops 8192 | bytes 65536 | tf_op jit(solution)/shard_map/psum | solution.py:63
  256.3 16.4 %reduce-scatter.10.cloned.1.call-done = f32[32,2048]{1,0:T(8,128)} async-done(((f32[32,8192]{1,0:T(8,128)}), f32[32,2048]{1,0:T(8,128)}) %reduce-scatter.10.cloned.1.call-update) | async-done | bytes 262160 | tf_op jit(solution)/shard_map/reduce_scatter | solution.py:60
  276.1 4.7 collective-permute-done.1
  282.5 65.4 %all-gather.11.cloned.1.call-done = bf16[512,2048]{1,0:T(8,128)(2,1)} async-done(((bf16[32,2048]{1,0:T(8,128)(2,1)}), bf16[512,2048]{1,0:T(8,128)(2,1)}) %all-gather.11.cloned.1.call-update) | async-done | bytes 2097168 | tf_op jit(solution)/shard_map/all_gather | solution.py:55
  350.7 23.8 %all_to_all.114 = f32[16,32,512]{2,1,0:T(8,128)S(1)} all-to-all(f32[16,32,512]{2,1,0:T(8,128)S(1)} %fusion.9), channel_id=1, replica_groups=mesh['dp'=16,'section'=4,'tensor'=4] {'dp'}, dimensions={0} | all-to-all | bytes 2097152 | tf_op jit(solution)/shard_map/all_to_all | solution.py:59
  377.4 13.2 %psum.114 = f32[32,256]{1,0:T(8,128)S(1)} all-reduce(f32[32,256]{1,0:T(8,128)S(1)} %fusion.50), channel_id=1, replica_groups=mesh['dp'=16,'section'=4,'tensor'=4] {'tensor'}, use_global_device_ids=true, to_apply=%region_5.6 | all-reduce | flops 8192 | bytes 65536 | tf_op jit(solution)/shard_map/psum | solution.py:63
  390.6 16.4 %reduce-scatter.12.cloned.1.call-done = f32[32,2048]{1,0:T(8,128)} async-done(((f32[32,8192]{1,0:T(8,128)}), f32[32,2048]{1,0:T(8,128)}) %reduce-scatter.12.cloned.1.call-update) | async-done | bytes 262160 | tf_op jit(solution)/shard_map/reduce_scatter | solution.py:60
  410.4 4.8 collective-permute-done.2
  416.8 65.4 %all-gather.13.cloned.1.call-done = bf16[512,2048]{1,0:T(8,128)(2,1)} async-done(((bf16[32,2048]{1,0:T(8,128)(2,1)}), bf16[512,2048]{1,0:T(8,128)(2,1)}) %all-gather.13.cloned.1.call-update) | async-done | bytes 2097168 | tf_op jit(solution)/shard_map/all_gather | solution.py:55
  485.0 23.8 %all_to_all.115 = f32[16,32,512]{2,1,0:T(8,128)S(1)} all-to-all(f32[16,32,512]{2,1,0:T(8,128)S(1)} %fusion.7), channel_id=1, replica_groups=mesh['dp'=16,'section'=4,'tensor'=4] {'dp'}, dimensions={0} | all-to-all | bytes 2097152 | tf_op jit(solution)/shard_map/all_to_all | solution.py:59
  512.3 13.2 %psum.115 = f32[32,256]{1,0:T(8,128)S(1)} all-reduce(f32[32,256]{1,0:T(8,128)S(1)} %fusion.48), channel_id=1, replica_groups=mesh['dp'=16,'section'=4,'tensor'=4] {'tensor'}, use_global_device_ids=true, to_apply=%region_7.8 | all-reduce | flops 8192 | bytes 65536 | tf_op jit(solution)/shard_map/psum | solution.py:63
  525.6 15.8 %reduce-scatter.14.cloned.1.call-done = f32[32,2048]{1,0:T(8,128)} async-done(((f32[32,8192]{1,0:T(8,128)}), f32[32,2048]{1,0:T(8,128)}) %reduce-scatter.14.cloned.1.call-update) | async-done | bytes 262160 | tf_op jit(solution)/shard_map/reduce_scatter | solution.py:60
  551.0 65.6 %all-gather.15.cloned.1.call-done = bf16[512,2048]{1,0:T(8,128)(2,1)} async-done(((bf16[32,2048]{1,0:T(8,128)(2,1)}), bf16[512,2048]{1,0:T(8,128)(2,1)}) %all-gather.15.cloned.1.call-update) | async-done | bytes 2097168 | tf_op jit(solution)/shard_map/all_gather | solution.py:55
  619.4 23.8 %all_to_all.116 = f32[16,32,512]{2,1,0:T(8,128)S(1)} all-to-all(f32[16,32,512]{2,1,0:T(8,128)S(1)} %fusion.5), channel_id=1, replica_groups=mesh['dp'=16,'section'=4,'tensor'=4] {'dp'}, dimensions={0} | all-to-all | bytes 2097152 | tf_op jit(solution)/shard_map/all_to_all | solution.py:59
  647.3 13.2 %psum.116 = f32[32,256]{1,0:T(8,128)S(1)} all-reduce(f32[32,256]{1,0:T(8,128)S(1)} %fusion.46), channel_id=1, replica_groups=mesh['dp'=16,'section'=4,'tensor'=4] {'tensor'}, use_global_device_ids=true, to_apply=%region_9.10 | all-reduce | flops 8192 | bytes 65536 | tf_op jit(solution)/shard_map/psum | solution.py:63
  660.6 15.0 %reduce-scatter.16.cloned.1.call-done = f32[32,2048]{1,0:T(8,128)} async-done(((f32[32,8192]{1,0:T(8,128)}), f32[32,2048]{1,0:T(8,128)}) %reduce-scatter.16.cloned.1.call-update) | async-done | bytes 262160 | tf_op jit(solution)/shard_map/reduce_scatter | solution.py:60
  685.1 65.8 %all-gather.17.cloned.1.call-done = bf16[512,2048]{1,0:T(8,128)(2,1)} async-done(((bf16[32,2048]{1,0:T(8,128)(2,1)}), bf16[512,2048]{1,0:T(8,128)(2,1)}) %all-gather.17.cloned.1.call-update) | async-done | bytes 2097168 | tf_op jit(solution)/shard_map/all_gather | solution.py:55
  753.7 23.7 %all_to_all.117 = f32[16,32,512]{2,1,0:T(8,128)S(1)} all-to-all(f32[16,32,512]{2,1,0:T(8,128)S(1)} %fusion.3), channel_id=1, replica_groups=mesh['dp'=16,'section'=4,'tensor'=4] {'dp'}, dimensions={0} | all-to-all | bytes 2097152 | tf_op jit(solution)/shard_map/all_to_all | solution.py:59
  786.6 13.3 %psum.117 = f32[32,256]{1,0:T(8,128)S(1)} all-reduce(f32[32,256]{1,0:T(8,128)S(1)} %fusion.44), channel_id=1, replica_groups=mesh['dp'=16,'section'=4,'tensor'=4] {'tensor'}, use_global_device_ids=true, to_apply=%region_11.12 | all-reduce | flops 8192 | bytes 65536 | tf_op jit(solution)/shard_map/psum | solution.py:63
  799.9 10.4 reduce-scatter.18.cloned.1.call-done
  822.3 46.5 %all-reduce.9.cloned.1.call-done = (f32[32,256]{1,0:T(8,128)}, f32[32,256]{1,0:T(8,128)}, f32[32,256]{1,0:T(8,128)}, f32[32,256]{1,0:T(8,128)}, f32[32,256]{1,0:...) async-done(((f32[32,256]{1,0:T(8,128)}, f32[32,256]{1,0:T(8,128)}, f32[32,256]{1,0:T(8,128)}, f32[32,256]{1,0:T(8,128)}, f32[32,256]{1,0:T(8,128)}, ...) | async-done | bytes 262160 | tf_op jit(solution)/shard_map/psum | solution.py:63
  880.2 57.4 %all-gather.19.cloned.1.call-done = bf16[512,2048]{1,0:T(8,128)(2,1)} async-done(((bf16[32,2048]{1,0:T(8,128)(2,1)}), bf16[512,2048]{1,0:T(8,128)(2,1)}) %all-gather.19.cloned.1.call-update) | async-done | bytes 2097168 | tf_op jit(solution)/shard_map/all_gather | solution.py:55
  948.6 19.1 %all-to-all-done.6 = f32[16,32,512]{2,1,0:T(8,128)} async-done(((f32[16,32,512]{2,1,0:T(8,128)}), f32[16,32,512]{2,1,0:T(8,128)}, u32[]{:S(2)}, u32[]{:S(2)}) %all-to-all-start.6) | async-done | bytes 1048608 | tf_op jit(solution)/shard_map/all_to_all | solution.py:59
  974.2 157.9 %all-reduce.5.cloned.1.call-done = f32[2048,16]{0,1:T(8,128)} async-done(((f32[2048,16]{0,1:T(8,128)}), f32[2048,16]{0,1:T(8,128)}) %all-reduce.5.cloned.1.call-update) | async-done | bytes 131088 | tf_op jit(solution)/shard_map/psum | solution.py:86
  1133.7 26.9 %reduce-scatter.20.cloned.1.call-done = f32[32,2048]{1,0:T(8,128)} async-done(((f32[32,8192]{1,0:T(8,128)}), f32[32,2048]{1,0:T(8,128)}) %reduce-scatter.20.cloned.1.call-update) | async-done | bytes 262160 | tf_op jit(solution)/shard_map/reduce_scatter | solution.py:60
  1162.7 65.5 %all-reduce.7.cloned.1.call-done = f32[4,32,2048]{2,1,0:T(8,128)} async-done(((f32[4,32,2048]{2,1,0:T(8,128)}), f32[4,32,2048]{2,1,0:T(8,128)}) %all-reduce.7.cloned.1.call-update) | async-done | bytes 1048592 | tf_op jit(solution)/shard_map/psum | solution.py:88
  (181 shorter events, 130.7 us)
Async XLA Ops:
  7.2 71.3 %copy-start = (bf16[1,2048,512]{2,1,0:T(8,128)(2,1)S(1)}, bf16[1,2048,512]{2,1,0:T(8,128)(2,1)}, u32[]{:S(2)}) copy-start(bf16[1,2048,512]{2,1,0:T(8,128)(2,1)} %param.10) | copy-start | bytes 6291460
  7.2 71.3 %all-gather.21.cloned.1.call-start = ((), (), s32[]{:S(2)}) async-start(), calls=%async_computation.29 | async-start | bytes 2228224 | tf_op jit(solution)/shard_map/all_gather | solution.py:55
  9.0 128.6 %reduce-scatter.8.cloned.1.call-start = ((), (), s32[]{:S(2)}) async-start(), calls=%async_computation.14 | async-start | bytes 1310720 | tf_op jit(solution)/shard_map/reduce_scatter | solution.py:60
  106.1 32.2 %copy-start.1 = (bf16[1,2048,256]{2,1,0:T(8,128)(2,1)S(1)}, bf16[1,2048,256]{2,1,0:T(8,128)(2,1)}, u32[]{:S(2)}) copy-start(bf16[1,2048,256]{2,1,0:T(8,128)(2,1)} %param.11) | copy-start | bytes 3145732
  106.2 107.4 %all-gather.9.cloned.1.call-start = ((), (), s32[]{:S(2)}) async-start(), calls=%async_computation.15 | async-start | bytes 2228224 | tf_op jit(solution)/shard_map/all_gather | solution.py:55
  140.4 6.0 collective-permute-start
  148.0 124.8 %reduce-scatter.10.cloned.1.call-start = ((), (), s32[]{:S(2)}) async-start(), calls=%async_computation.16 | async-start | bytes 1310720 | tf_op jit(solution)/shard_map/reduce_scatter | solution.py:60
  241.3 106.6 %all-gather.11.cloned.1.call-start = ((), (), s32[]{:S(2)}) async-start(), calls=%async_computation.17 | async-start | bytes 2228224 | tf_op jit(solution)/shard_map/all_gather | solution.py:55
  274.8 6.0 collective-permute-start.1
  282.5 124.5 %reduce-scatter.12.cloned.1.call-start = ((), (), s32[]{:S(2)}) async-start(), calls=%async_computation.18 | async-start | bytes 1310720 | tf_op jit(solution)/shard_map/reduce_scatter | solution.py:60
  375.6 106.6 %all-gather.13.cloned.1.call-start = ((), (), s32[]{:S(2)}) async-start(), calls=%async_computation.19 | async-start | bytes 2228224 | tf_op jit(solution)/shard_map/all_gather | solution.py:55
  409.1 6.1 collective-permute-start.2
  416.8 124.6 %reduce-scatter.14.cloned.1.call-start = ((), (), s32[]{:S(2)}) async-start(), calls=%async_computation.20 | async-start | bytes 1310720 | tf_op jit(solution)/shard_map/reduce_scatter | solution.py:60
  509.9 106.6 %all-gather.15.cloned.1.call-start = ((), (), s32[]{:S(2)}) async-start(), calls=%async_computation.21 | async-start | bytes 2228224 | tf_op jit(solution)/shard_map/all_gather | solution.py:55
  543.5 5.9 collective-permute-start.3
  550.9 124.7 %reduce-scatter.16.cloned.1.call-start = ((), (), s32[]{:S(2)}) async-start(), calls=%async_computation.22 | async-start | bytes 1310720 | tf_op jit(solution)/shard_map/reduce_scatter | solution.py:60
  644.2 106.7 %all-gather.17.cloned.1.call-start = ((), (), s32[]{:S(2)}) async-start(), calls=%async_computation.23 | async-start | bytes 2228224 | tf_op jit(solution)/shard_map/all_gather | solution.py:55
  677.7 5.7 collective-permute-start.4
  685.1 125.2 %reduce-scatter.18.cloned.1.call-start = ((), (), s32[]{:S(2)}) async-start(), calls=%async_computation.24 | async-start | bytes 1310720 | tf_op jit(solution)/shard_map/reduce_scatter | solution.py:60
  778.6 90.3 %all-reduce.9.cloned.1.call-start = ((), (), s32[]{:S(2)}) async-start(), calls=%async_computation.30 | async-start | bytes 524288 | tf_op jit(solution)/shard_map/psum | solution.py:63
  799.9 21.9 %copy-start.13 = (f32[32,256]{1,0:T(8,128)}, f32[32,256]{1,0:T(8,128)S(1)}, u32[]{:S(2)}) copy-start(f32[32,256]{1,0:T(8,128)S(1)} %psum.117) | copy-start | bytes 98308
  812.4 6.1 collective-permute-start.5
  821.8 115.9 %all-gather.19.cloned.1.call-start = ((), (), s32[]{:S(2)}) async-start(), calls=%async_computation.25 | async-start | bytes 2228224 | tf_op jit(solution)/shard_map/all_gather | solution.py:55
  941.5 4.5 copy-start.18
  941.5 26.2 %all-to-all-start.6 = ((f32[16,32,512]{2,1,0:T(8,128)}), f32[16,32,512]{2,1,0:T(8,128)}, u32[]{:S(2)}, u32[]{:S(2)}) async-start(f32[16,32,512]{2,1,0:T(8,128)} %fusion.1), calls=%async_computation.12 | async-start | bytes 2097152 | tf_op jit(solution)/shard_map/all_to_all | solution.py:59
  945.9 186.2 %all-reduce.5.cloned.1.call-start = ((), (), s32[]{:S(2)}) async-start(), calls=%async_computation.27 | async-start | bytes 262144 | tf_op jit(solution)/shard_map/psum | solution.py:86
  946.2 24.0 %copy-start.15 = (f32[2048,16]{0,1:T(8,128)S(1)}, f32[2048,16]{0,1:T(8,128)}, u32[]{:S(2)}) copy-start(f32[2048,16]{0,1:T(8,128)} %param.15) | copy-start | bytes 393220
  946.3 25.9 %copy-start.12 = (f32[4,32,16]{1,2,0:T(8,128)}, f32[4,32,16]{1,2,0:T(8,128)S(1)}, u32[]{:S(2)}) copy-start(f32[4,32,16]{1,2,0:T(8,128)S(1)} %constant_dynamic-update-slice_fusion.5) | copy-start | bytes 24580
  948.6 212.1 %reduce-scatter.20.cloned.1.call-start = ((), (), s32[]{:S(2)}) async-start(), calls=%async_computation.26 | async-start | bytes 1310720 | tf_op jit(solution)/shard_map/reduce_scatter | solution.py:60
  970.0 190.6 %copy-start.4 = (bf16[32,2048]{1,0:T(8,128)(2,1)S(1)}, bf16[32,2048]{1,0:T(8,128)(2,1)}, u32[]{:S(2)}) copy-start(bf16[32,2048]{1,0:T(8,128)(2,1)} %copy-done.3) | copy-start | bytes 393220
  970.0 190.6 %copy-start.16 = (f32[32,256]{1,0:T(8,128)S(1)}, f32[32,256]{1,0:T(8,128)}, u32[]{:S(2)}) copy-start(f32[32,256]{1,0:T(8,128)} %get-tuple-element.4) | copy-start | bytes 98308
  970.0 258.2 %all-reduce.7.cloned.1.call-start = ((), (), s32[]{:S(2)}) async-start(), calls=%async_computation.28 | async-start | bytes 2097152 | tf_op jit(solution)/shard_map/psum | solution.py:88
  (13 other events, 28.2 us)
Sparse Core Ops, SparseCore 0:
  11.3 67.1 all-gather.20
  106.3 31.1 reduce-scatter.7
  148.1 65.4 all-gather.8
  241.4 31.2 reduce-scatter.9
  282.6 65.2 all-gather.10
  375.7 31.2 reduce-scatter.11
  416.9 65.2 all-gather.12
  510.0 31.2 reduce-scatter.13
  551.0 65.4 all-gather.14
  644.3 31.2 reduce-scatter.15
  685.2 65.6 all-gather.16
  778.7 31.5 reduce-scatter.17
  821.9 46.9 all-reduce.8
  871.7 65.8 all-gather.18
  949.8 182.2 all-reduce.4
  1135.1 25.4 reduce-scatter.19
  1163.4 64.8 all-reduce.6
where the time goes:
time: 1240 us
  waiting for transfers between devices  887 us (72%)
  blocking collectives  222 us (18%)
  matrix products  59.6 us (5%)
  local copies, waits for them, and re-layouts  20.4 us (2%)
  other arithmetic  20.3 us (2%)
  between operations  14.5 us (1%)
  starting transfers between devices  13 us (1%)
    all_gather x7, waiting for transfers between devices, on_device(): lax.all_gather(incoming, 'dp', axis=0, tiled=True)  455 us
    psum x1, waiting for transfers between devices, on_device(): head_grad = lax.psum(local_head, 'dp') * (1.0 / math.sqrt(total))  158 us
    all_to_all x6, blocking collectives, on_device(): lax.all_to_all(partial_block, 'dp', split_axis=0, concat_axis=1, tiled=True)  143 us
    reduce_scatter x7, waiting for transfers between devices, on_device(): base = lax.psum_scatter(spread, 'tensor', scatter_dimension=1, tiled=True)  117 us
    psum x6, blocking collectives, on_device(): down_full, back_full = lax.psum((down_part, back_part), 'tensor')  79.5 us
    psum x1, waiting for transfers between devices, on_device(): lax.psum(partial_hidden, 'section').reshape(micro, rows, width)  65.5 us
    psum x1, waiting for transfers between devices, on_device(): down_full, back_full = lax.psum((down_part, back_part), 'tensor')  46.5 us
    ppermute x6, waiting for transfers between devices, from_behind(): lax.ppermute(value, axis, [(source, source + steps) for source in range(f...  26.2 us
  transfers between devices with their start and end apart: 24, of which 24 were waited for; matrix products, arithmetic and copies ran while one was open for 4% of the time, Pallas kernels for 0%

commit v1 on v0

v1 whole, which is shorter than its diff:
```python
import functools
import math

import jax
import jax.numpy as jnp
from jax import lax
from jax.experimental import pallas as pl
from jax.experimental.pallas import tpu as pltpu
from jax.sharding import PartitionSpec as P

BF = jnp.bfloat16
F32 = jnp.float32
NT_DIMS = (((1,), (1,)), ((), ()))
SUBS = 4
TOK = 16


def dot_nt(a, b, precision=None):
    return lax.dot_general(a, b, NT_DIMS, precision=precision, preferred_element_type=F32)


def kernel(
    sizes,
    u, hid, w, a, b, st, states, ct,
    out, scale, head, hidden,
    g, pb, rx, own, sp, se, sb, sall, ai, dx, bx, pacc, bacc, cta, sga, hl, hx, ho,
    r_s, r_z, r_y, r_c, r_x,
    s_s, s_z, s_c, s_x, s_p, s_o, s_b, s_u,
    r_one, s_one,
):
    X, Y, S, DP, N, R = sizes
    T = TOK
    FB = w.shape[1]
    ex = scale.shape[1]
    rank = R // ex
    d = lax.axis_index("dp")
    sec = lax.axis_index("section")
    x = lax.axis_index("tensor")
    y = d // SUBS
    m = d % SUBS
    zh = m // 2
    core = m % 2

    def dev(dp=None, section=None, tensor=None):
        return {
            "dp": d if dp is None else dp,
            "section": sec if section is None else section,
            "tensor": x if tensor is None else tensor,
        }

    def send(src, dst, ssem, rsem, target):
        pltpu.make_async_remote_copy(
            src_ref=src, dst_ref=dst, send_sem=ssem, recv_sem=rsem,
            device_id=target, device_id_type=pl.DeviceIdType.MESH,
        ).start()

    def wait(ref, sem):
        pltpu.make_async_copy(ref, ref, sem).wait()

    def cols(index, width):
        return pl.ds(pl.multiple_of(index * width, 128), width)

    def rows(index, height):
        return pl.ds(pl.multiple_of(index * height, 16), height)

    same = x == y
    apart = jnp.logical_not(same)
    top = sec == S - 1
    bottom = sec == 0

    barrier = pltpu.get_barrier_semaphore()

    def hello(target):
        pl.semaphore_signal(barrier, inc=1, device_id=target, device_id_type=pl.DeviceIdType.MESH)

    for j in range(1, DP):
        hello(dev(dp=(d + j) % DP))
    for j in range(1, X):
        hello(dev(tensor=(x + j) % X))
    for j in range(1, S):
        hello(dev(section=(sec + j) % S))

    @pl.when(apart)
    def _():
        for o in range(SUBS):
            hello(dev(dp=x * SUBS + o, tensor=y))

        @pl.when(sec > 0)
        def _():
            hello(dev(dp=x * SUBS + m, section=sec - 1, tensor=y))

        @pl.when(sec < S - 1)
        def _():
            hello(dev(dp=x * SUBS + m, section=sec + 1, tensor=y))

    extra = SUBS + jnp.where(bottom, 0, 1) + jnp.where(top, 0, 1)
    pl.semaphore_wait(barrier, DP - 1 + X - 1 + S - 1 + jnp.where(same, 0, extra))

    @pl.when(top)
    def _():
        @pl.loop(0, N)
        def _(k):
            for j in range(1, SUBS):
                o = (m + j) % SUBS
                send(u.at[k, :, cols(o, FB)], g.at[k, o % 2, y, o // 2, m],
                     s_u.at[k], r_s.at[k], dev(dp=y * SUBS + o))
            pltpu.make_async_copy(u.at[k, :, cols(m, FB)], g.at[k, core, y, zh, m], r_s.at[k]).start()

    s_full = st[...]
    s_hi = s_full.astype(BF)
    s_lo = (s_full - s_hi.astype(F32)).astype(BF)
    both = jnp.concatenate([s_hi, s_lo], axis=0)
    sb[...] = both
    sall[d] = both
    for j in range(1, DP):
        send(sb, sall.at[d], s_one.at[0], r_one.at[0], dev(dp=(d + j) % DP))

    @pl.when(apart)
    def _():
        send(a.at[rows(m, FB)], ai, s_one.at[1], r_one.at[1], dev(dp=x * SUBS + m, tensor=y))

    @pl.when(same)
    def _():
        pltpu.make_async_copy(a.at[rows(m, FB)], ai, r_one.at[1]).start()

    cta[sec] = ct[...]
    for j in range(1, S):
        send(ct, cta.at[sec], s_one.at[2], r_one.at[2], dev(section=(sec + j) % S))

    def step_s(k):
        mine = g.at[k, core, y, zh]
        wait(mine, r_s.at[k])
        send(mine, mine, s_s.at[k], r_z.at[k], dev(dp=(d + 2) % SUBS + y * SUBS))
        for j in range(1, Y):
            send(mine, mine, s_s.at[k], r_y.at[k], dev(dp=((y + j) % Y) * SUBS + m))

    def step_z(k):
        theirs = g.at[k, core, y, 1 - zh]
        wait(theirs, r_z.at[k])
        for j in range(1, Y):
            send(theirs, theirs, s_z.at[k], r_y.at[k], dev(dp=((y + j) % Y) * SUBS + m))

    def prepare():
        down = jnp.dot(hid[...], a[...], preferred_element_type=F32)
        dx[x] = down
        for j in range(1, X):
            send(dx.at[x], dx.at[x], s_one.at[3], r_one.at[3], dev(tensor=(x + j) % X))
        wait(sall.at[pl.ds(0, DP - 1)], r_one.at[0])
        expert = lax.broadcasted_iota(jnp.int32, (2 * ex, R), 0)
        column = lax.broadcasted_iota(jnp.int32, (2 * ex, R), 1)
        expand = jnp.where(lax.rem(expert, ex) == lax.div(column, rank), 1.0, 0.0).astype(BF)

        @pl.loop(0, DP)
        def _(owner):
            turned = sall[owner].astype(F32).T.astype(BF)
            se[owner] = jnp.dot(turned, expand, preferred_element_type=F32)

        wait(ai, r_one.at[1])

    def half(k, c):
        total = None
        back = None
        for zz in range(2):
            f = zz * 2 + c
            left = g[k, c, :, zz].reshape(Y * SUBS * T, FB)
            t = jnp.dot(left, w[rows(f, FB), :], preferred_element_type=F32)
            q = dot_nt(left, b[:, cols(f, FB)])
            total = t if total is None else total + t
            back = q if back is None else back + q
        return total, back

    def step_m(k):
        wait(g.at[k, 0, pl.ds(0, Y - 1)], r_y.at[k])
        send(g.at[k, core], g.at[k, core], s_c.at[k], r_c.at[k], dev(dp=d + 1 - 2 * core))
        total, back = half(k, core)
        pacc[...] = total
        bacc[...] = back
        wait(g.at[k, 0], r_c.at[k])

        @pl.when(sec < S - 1)
        def _():
            send(g.at[k, :, y, :, m], out.at[k], s_o.at[k], r_one.at[4], dev(section=sec + 1))

        total, back = half(k, 1 - core)
        back = bacc[...] + back
        bacc[...] = back
        spread = se[:, rows(k, T), :].reshape(DP * T, R)
        weighted = (back * spread).astype(BF)
        pacc[...] += total + dot_nt(weighted, ai[...])

        @pl.when(same)
        def _():
            pacc[...] += g[k, core, :, zh].reshape(Y * SUBS * T, FB).astype(F32)

        pb[k] = pacc[...].astype(BF).reshape(Y, SUBS, T, FB)
        for j in range(1, X):
            r = (x + j) % X
            send(pb.at[k, r], rx.at[k, x], s_x.at[k], r_x.at[k], dev(tensor=r))
        own[k] = pacc[rows(x, SUBS * T), :]
        bx[x, k] = bacc[rows(d, T), :]
        for j in range(1, X):
            send(bx.at[x, k], bx.at[x, k], s_b.at[k], r_one.at[5], dev(tensor=(x + j) % X))

    def step_x(k):
        wait(rx.at[k, pl.ds(0, X - 1)], r_x.at[k])
        total = own[k]
        for j in range(1, X):
            total = total + rx[k, (x + j) % X].reshape(SUBS * T, FB).astype(F32)
        sp[k] = total.astype(BF).reshape(SUBS, T, FB)

        @pl.when(sec > 0)
        def _():
            send(sp.at[k], g.at[k, core, x, zh], s_p.at[k], r_s.at[k],
                 dev(dp=x * SUBS + m, section=sec - 1, tensor=y))

        @pl.when(bottom)
        def _():
            for o in range(SUBS):
                here = jnp.logical_and(same, m == o)

                @pl.when(here)
                def _():
                    pltpu.make_async_copy(sp.at[k, o], out.at[k, core, zh], r_one.at[4]).start()

                @pl.when(jnp.logical_not(here))
                def _():
                    send(sp.at[k, o], out.at[k, core, zh], s_p.at[k], r_one.at[4],
                         dev(dp=x * SUBS + o, tensor=y))

    @pl.loop(0, N + 2)
    def _(i):
        @pl.when(i < N)
        def _():
            step_s(i)

        @pl.when(i >= 2)
        def _():
            step_x(i - 2)

        @pl.when(i < N)
        def _():
            step_z(i)

        @pl.when(i == 1)
        def _():
            prepare()

        @pl.when(jnp.logical_and(i >= 1, i < N + 1))
        def _():
            step_m(i - 1)

    wait(bx.at[pl.ds(0, X - 1)], r_one.at[5])
    wait(dx.at[pl.ds(0, X - 1)], r_one.at[3])
    back = bx[0].reshape(N * T, R)
    down = dx[0]
    for j in range(1, X):
        back = back + bx[j].reshape(N * T, R)
        down = down + dx[j]
    product = down * back
    expert = lax.broadcasted_iota(jnp.int32, (ex, R), 0)
    column = lax.broadcasted_iota(jnp.int32, (ex, R), 1)
    group = jnp.where(expert == lax.div(column, rank), 1.0, 0.0).astype(F32)
    scale[...] = dot_nt(product, group, lax.Precision.HIGHEST)
    turned = dot_nt(group, product, lax.Precision.HIGHEST)
    sga[sec] = turned
    for j in range(1, S):
        send(sga.at[sec], sga.at[sec], s_one.at[5], r_one.at[6], dev(section=(sec + j) % S))

    t_hi = turned.astype(BF)
    t_lo = (turned - t_hi.astype(F32)).astype(BF)
    hl[...] = (jnp.dot(t_hi, states[...], preferred_element_type=F32)
               + jnp.dot(t_lo, states[...], preferred_element_type=F32))
    FD = hl.shape[1] // DP
    for j in range(1, DP):
        e = (d + j) % DP
        send(hl.at[:, cols(e, FD)], hx.at[d], s_one.at[6], r_one.at[7], dev(dp=e))
    hx[d] = hl[:, cols(d, FD)]
    wait(hx.at[pl.ds(0, DP - 1)], r_one.at[7])
    total = hx[0]
    for j in range(1, DP):
        total = total + hx[j]
    total = total * (1.0 / math.sqrt(N * T * DP))
    ho[...] = total
    head[:, cols(d, FD)] = total
    for j in range(1, DP):
        send(ho, head.at[:, cols(d, FD)], s_one.at[7], r_one.at[8], dev(dp=(d + j) % DP))

    wait(cta.at[pl.ds(0, S - 1)], r_one.at[2])
    wait(sga.at[pl.ds(0, S - 1)], r_one.at[6])
    left = sga[...].reshape(S * ex, N * T).T
    right = cta[...].reshape(S * ex, -1)
    hidden[...] = jnp.dot(left, right, precision=lax.Precision.HIGHEST, preferred_element_type=F32)

    wait(hx.at[pl.ds(0, DP - 1)], r_one.at[8])
    wait(out, r_one.at[4])
    wait(sall.at[pl.ds(0, DP - 1)], s_one.at[0])

    @pl.when(apart)
    def _():
        wait(ai, s_one.at[1])

    wait(cta.at[pl.ds(0, S - 1)], s_one.at[2])
    wait(dx.at[pl.ds(0, X - 1)], s_one.at[3])
    wait(sga.at[pl.ds(0, S - 1)], s_one.at[5])
    wait(hx.at[pl.ds(0, DP - 1)], s_one.at[6])
    wait(hx.at[pl.ds(0, DP - 1)], s_one.at[7])

    @pl.loop(0, N)
    def _(k):
        wait(g.at[k, 0, :, 0], s_s.at[k])
        wait(g.at[k, 0, pl.ds(0, Y - 1), 0], s_z.at[k])
        wait(g.at[k, 0], s_c.at[k])
        wait(rx.at[k, pl.ds(0, X - 1)], s_x.at[k])
        wait(bx.at[pl.ds(0, X - 1), k], s_b.at[k])

        @pl.when(top)
        def _():
            wait(sp.at[k, pl.ds(0, SUBS - 1)], s_u.at[k])

        @pl.when(sec > 0)
        def _():
            wait(sp.at[k], s_p.at[k])

        @pl.when(jnp.logical_and(bottom, apart))
        def _():
            wait(sp.at[k], s_p.at[k])

        @pl.when(jnp.logical_and(bottom, same))
        def _():
            wait(sp.at[k, pl.ds(0, SUBS - 1)], s_p.at[k])

        @pl.when(sec < S - 1)
        def _():
            wait(out.at[k], s_o.at[k])


def on_device(u, saved, w, a, b, mix, states, classifier):
    X, S, DP = (lax.axis_size(n) for n in ("tensor", "section", "dp"))
    Y = DP // SUBS
    micro, per, F = u.shape
    T = TOK
    N = micro * per // T
    FB = w.shape[2]
    R = a.shape[2]
    ex = mix.shape[2]
    tokens = N * T
    vmem = pl.BlockSpec(memory_space=pltpu.VMEM)
    dma = pltpu.SemaphoreType.DMA
    sizes = (X, Y, S, DP, N, R)
    out, scale, head, hidden = pl.pallas_call(
        functools.partial(kernel, sizes),
        out_shape=(
            jax.ShapeDtypeStruct((N, 2, 2, T, FB), BF),
            jax.ShapeDtypeStruct((tokens, ex), F32),
            jax.ShapeDtypeStruct((ex, F), F32),
            jax.ShapeDtypeStruct((tokens, F), F32),
        ),
        in_specs=[vmem] * 8,
        out_specs=(vmem,) * 4,
        scratch_shapes=[
            pltpu.VMEM((N, 2, Y, 2, SUBS, T, FB), BF),
            pltpu.VMEM((N, Y, SUBS, T, FB), BF),
            pltpu.VMEM((N, X, SUBS, T, FB), BF),
            pltpu.VMEM((N, SUBS * T, FB), F32),
            pltpu.VMEM((N, SUBS, T, FB), BF),
            pltpu.VMEM((DP, tokens, R), F32),
            pltpu.VMEM((2 * ex, tokens), BF),
            pltpu.VMEM((DP, 2 * ex, tokens), BF),
            pltpu.VMEM((FB, R), BF),
            pltpu.VMEM((X, tokens, R), F32),
            pltpu.VMEM((X, N, T, R), F32),
            pltpu.VMEM((Y * SUBS * T, FB), F32),
            pltpu.VMEM((Y * SUBS * T, R), F32),
            pltpu.VMEM((S, ex, F), F32),
            pltpu.VMEM((S, ex, tokens), F32),
            pltpu.VMEM((ex, F), F32),
            pltpu.VMEM((DP, ex, F // DP), F32),
            pltpu.VMEM((ex, F // DP), F32),
        ] + [dma((N,))] * 13 + [dma((9,)), dma((8,))],
        compiler_params=pltpu.CompilerParams(
            collective_id=0, has_side_effects=True, vmem_limit_bytes=48 * 1024 * 1024,
        ),
    )(
        u.reshape(N, T, F),
        saved.reshape(tokens, F),
        w[0], a[0], b[0],
        mix.reshape(tokens, ex).T,
        states.reshape(tokens, F),
        classifier.T,
    )
    grads = out.reshape(micro, per // T, 2, 2, T, FB).transpose(0, 1, 4, 3, 2, 5).reshape(1, micro, per, F)
    return grads, scale.reshape(micro, per, ex), head.T, hidden.reshape(micro, per, F)


def solution(mesh):
    return jax.shard_map(
        on_device,
        mesh=mesh,
        in_specs=(
            P(None, "dp", "tensor"),
            P("section", None, "dp", "tensor"),
            P("section", "tensor", "dp"),
            P("section", "tensor", None),
            P("section", None, "tensor"),
            P(None, "dp", "section"),
            P(None, "dp", "tensor"),
            P("tensor", "section"),
        ),
        out_specs=(
            P("section", None, "dp", "tensor"),
            P(None, "dp", "section"),
            P("tensor", "section"),
            P(None, "dp", "tensor"),
        ),
        check_vma=False,
    )
```

time: 1240 us -> 249 us (0.20)
  waiting for transfers between devices: 887 us -> 0 us
  Pallas kernels: 0 us -> 237 us
  blocking collectives: 222 us -> 0 us
  matrix products: 59.6 us -> 0 us
  other arithmetic: 20.3 us -> 0 us
  between operations: 14.5 us -> 0.66 us
  starting transfers between devices: 13 us -> 0 us
    all_gather x7 -> x0, waiting for transfers between devices: 455 us -> none  [on_device(): lax.all_gather(incoming, 'dp', axis=0, tiled=True)]
    psum x3 -> x0, waiting for transfers between devices: 270 us -> none  [the longest x1 158 us: on_device(): head_grad = lax.psum(local_head, 'dp') * (1.0 / math.sqrt(total))]
    pallas_call x0 -> x1, Pallas kernels: none -> 237 us  [on_device(): pl.pallas_call(functools.partial(kernel, sizes), out_shape=(jax.ShapeDtyp...]
    all_to_all x6 -> x0, blocking collectives: 143 us -> none  [on_device(): lax.all_to_all(partial_block, 'dp', split_axis=0, concat_axis=1, tiled=True)]
    reduce_scatter x7 -> x0, waiting for transfers between devices: 117 us -> none  [on_device(): base = lax.psum_scatter(spread, 'tensor', scatter_dimension=1, tiled=True)]
    psum x6 -> x0, blocking collectives: 79.5 us -> none  [on_device(): down_full, back_full = lax.psum((down_part, back_part), 'tensor')]
    dot_general x30 -> x0, matrix products: 59.6 us -> none  [the longest x7 20.8 us: on_device(): jnp.dot(lax.all_gather(incoming, 'dp', axis=0, tiled=True), block, prefer...]
    ppermute x6 -> x0, waiting for transfers between devices: 26.2 us -> none  [from_behind(): lax.ppermute(value, axis, [(source, source + steps) for source in range(f...]
  transfers between devices with their start and end apart: 24 -> 0, of which waited for: 24 -> 0; matrix products, arithmetic and copies ran while one was open for 4% -> 0% of each run, Pallas kernels for 0% -> 0%
where the time goes in v1:
time: 249 us
  Pallas kernels  237 us (95%)
  local copies, waits for them, and re-layouts  11.4 us (5%)
    pallas_call x1, Pallas kernels, on_device(): pl.pallas_call(functools.partial(kernel, sizes), out_shape=(jax.ShapeDtyp...  237 us
    unnamed x16, local copies, waits for them, and re-layouts  9.57 us

profile of v1, /device:TPU:1, one launch (start us, length us, event | category | flops | bytes accessed | tf_op | source)
XLA Modules:
  0.0 248.8 jit_solution(12033265438171362101)
XLA Ops:
  0.6 0.8 copy.12
  1.4 0.1 reshape.34
  1.5 0.0 copy-start
  1.5 1.2 copy-done
  2.7 0.0 copy-start.1
  2.7 1.2 copy-done.1
  3.9 0.0 copy-start.2
  3.9 1.0 copy-done.2
  5.0 0.0 copy-start.3
  5.0 1.0 copy-done.3
  6.0 0.0 copy-start.4
  6.0 1.0 copy-done.4
  7.1 0.0 copy-start.5
  7.1 0.9 copy-done.5
  8.0 236.8 %shard_map.111 = (bf16[8,2,2,16,512]{4,3,2,1,0:T(8,128)(2,1)S(1)}, f32[128,16]{1,0:T(8,128)S(1)}, f32[16,2048]{1,0:T(8,128)S(1)}, f32[128,2048]{1,0:T(8,128)S(1)}) custom-call(bf16[8,16,2048]{2,1,0:T(8,128)(2,1)S(1)} %bitcast.19, bf16[128,2048]{1,0:T(8,128)(2,1)S(1)} %bitcast.20, bf16[2048,512]{1,0:T(8,128)(2,1)} %bitcast.27, ...), custom_call_target="tpu_custom_call" | custom-call | tf_op jit(solution)/shard_map/pallas_call | solution.py:350
  244.8 0.5 copy.13
  245.3 1.2 reshape.37
  246.5 0.7 copy.14
  247.2 0.7 copy.17
  247.9 1.0 copy.18
Async XLA Ops:
  1.5 1.2 copy-start
  2.7 1.2 copy-start.1
  3.9 1.0 copy-start.2
  5.0 1.0 copy-start.3
  6.0 1.0 copy-start.4
  7.1 0.9 copy-start.5

commit v2 on v1

v2 whole, which is shorter than its diff:
```python
import functools
import math

import jax
import jax.numpy as jnp
from jax import lax
from jax.experimental import pallas as pl
from jax.experimental.pallas import tpu as pltpu
from jax.sharding import PartitionSpec as P

BF = jnp.bfloat16
F32 = jnp.float32
NT_DIMS = (((1,), (1,)), ((), ()))
SUBS = 4
TOK = 16
OWNERS = 2
ORDER = (("S", 0), ("M", 3), ("Z", 1), ("X", 4))


def dot_nt(a, b, precision=None):
    return lax.dot_general(a, b, NT_DIMS, precision=precision, preferred_element_type=F32)


def kernel(
    sizes,
    u, hid_in, w_in, a_in, b_in, mix_in, states_in, ct,
    out, scale, head, hidden,
    uv, us, hid, w, a, b, mix, states,
    g, pb, rx, own, sp, se, sb, sall, ai, dx, bx, pacc, bacc, cta, sga, hl, hx, hg,
    r_s, r_z, r_y, r_c, r_x,
    s_s, s_z, s_c, s_x, s_p, s_o, s_b, s_u,
    r_one, s_one, l_one,
):
    X, Y, S, DP, N, R = sizes
    T = TOK
    FB = w.shape[1]
    ex = mix.shape[1]
    rank = R // ex
    parts = SUBS // OWNERS
    d = lax.axis_index("dp")
    sec = lax.axis_index("section")
    x = lax.axis_index("tensor")
    y = d // SUBS
    m = d % SUBS
    zh = m // 2
    core = m % 2
    place = m % OWNERS

    def dev(dp=None, section=None, tensor=None):
        return {
            "dp": d if dp is None else dp,
            "section": sec if section is None else section,
            "tensor": x if tensor is None else tensor,
        }

    def send(src, dst, ssem, rsem, target):
        pltpu.make_async_remote_copy(
            src_ref=src, dst_ref=dst, send_sem=ssem, recv_sem=rsem,
            device_id=target, device_id_type=pl.DeviceIdType.MESH,
        ).start()

    def wait(ref, sem):
        pltpu.make_async_copy(ref, ref, sem).wait()

    def cols(index, width):
        return pl.ds(pl.multiple_of(index * width, 128), width)

    def rows(index, height):
        return pl.ds(pl.multiple_of(index * height, 16), height)

    def mine(k):
        return m // OWNERS == k % parts

    same = x == y
    apart = jnp.logical_not(same)
    top = sec == S - 1
    bottom = sec == 0

    @pl.when(top)
    def _():
        pltpu.make_async_copy(u, uv, l_one.at[6]).start()

    loads = ((mix_in, mix), (w_in, w), (b_in, b), (hid_in, hid), (a_in, a), (states_in, states))
    for i, (far, near) in enumerate(loads):
        pltpu.make_async_copy(far, near, l_one.at[i]).start()

    barrier = pltpu.get_barrier_semaphore()

    def hello(target):
        pl.semaphore_signal(barrier, inc=1, device_id=target, device_id_type=pl.DeviceIdType.MESH)

    for j in range(1, DP):
        hello(dev(dp=(d + j) % DP))
    for j in range(1, X):
        hello(dev(tensor=(x + j) % X))
    for j in range(1, S):
        hello(dev(section=(sec + j) % S))

    @pl.when(apart)
    def _():
        for o in range(SUBS):
            hello(dev(dp=x * SUBS + o, tensor=y))

        @pl.when(sec > 0)
        def _():
            hello(dev(dp=x * SUBS + m, section=sec - 1, tensor=y))

        @pl.when(sec < S - 1)
        def _():
            hello(dev(dp=x * SUBS + m, section=sec + 1, tensor=y))

    extra = SUBS + jnp.where(bottom, 0, 1) + jnp.where(top, 0, 1)
    pl.semaphore_wait(barrier, DP - 1 + X - 1 + S - 1 + jnp.where(same, 0, extra))

    @pl.when(top)
    def _():
        wait(uv, l_one.at[6])

        @pl.loop(0, N // parts)
        def _(kk):
            k = kk * parts + m // OWNERS
            for o in range(SUBS):
                us[kk, o] = uv[kk, :, o * FB:(o + 1) * FB]
            pltpu.make_async_copy(us.at[kk, m], g.at[k, core, y, zh, place], r_s.at[k]).start()
            for j in range(1, SUBS):
                o = (m + j) % SUBS
                send(us.at[kk, o], g.at[k, o % 2, y, o // 2, place],
                     s_u.at[k], r_s.at[k], dev(dp=y * SUBS + o))

    wait(mix, l_one.at[0])
    s_full = jnp.concatenate([mix[i] for i in range(mix.shape[0])], axis=1)
    s_hi = s_full.astype(BF)
    s_lo = (s_full - s_hi.astype(F32)).astype(BF)
    both = jnp.concatenate([s_hi, s_lo], axis=0)
    sb[...] = both
    sall[d] = both
    for j in range(1, DP):
        send(sb, sall.at[d], s_one.at[0], r_one.at[0], dev(dp=(d + j) % DP))

    @pl.when(apart)
    def _():
        send(a_in.at[rows(m, FB)], ai, s_one.at[1], r_one.at[1], dev(dp=x * SUBS + m, tensor=y))

    @pl.when(same)
    def _():
        pltpu.make_async_copy(a_in.at[rows(m, FB)], ai, r_one.at[1]).start()

    pltpu.make_async_copy(ct, cta.at[sec], r_one.at[2]).start()
    for j in range(1, S):
        send(ct, cta.at[sec], s_one.at[2], r_one.at[2], dev(section=(sec + j) % S))

    def step_s(k):
        block = g.at[k, core, y, zh]
        wait(block, r_s.at[k])
        send(block, block, s_s.at[k], r_z.at[k], dev(dp=(d + 2) % SUBS + y * SUBS))
        for j in range(1, Y):
            send(block, block, s_s.at[k], r_y.at[k], dev(dp=((y + j) % Y) * SUBS + m))

    def step_z(k):
        block = g.at[k, core, y, 1 - zh]
        wait(block, r_z.at[k])
        for j in range(1, Y):
            send(block, block, s_z.at[k], r_y.at[k], dev(dp=((y + j) % Y) * SUBS + m))

    def prepare():
        wait(hid, l_one.at[3])
        wait(a, l_one.at[4])
        down = jnp.dot(hid[...], a[...], preferred_element_type=F32)
        dx[x] = down
        for j in range(1, X):
            send(dx.at[x], dx.at[x], s_one.at[3], r_one.at[3], dev(tensor=(x + j) % X))
        wait(sall.at[pl.ds(0, DP - 1)], r_one.at[0])
        expert = lax.broadcasted_iota(jnp.int32, (2 * ex, R), 0)
        column = lax.broadcasted_iota(jnp.int32, (2 * ex, R), 1)
        expand = jnp.where(lax.rem(expert, ex) == lax.div(column, rank), 1.0, 0.0).astype(BF)

        @pl.loop(0, DP)
        def _(owner):
            turned = sall[owner].astype(F32).T.astype(BF)
            se[owner // SUBS, owner % SUBS] = jnp.dot(turned, expand, preferred_element_type=F32)

        wait(ai, r_one.at[1])
        wait(w, l_one.at[1])
        wait(b, l_one.at[2])

    def half(k, c):
        total = None
        back = None
        for zz in range(2):
            f = zz * 2 + c
            left = g[k, c, :, zz].reshape(Y * OWNERS * T, FB)
            t = jnp.dot(left, w[rows(f, FB), :], preferred_element_type=F32)
            q = dot_nt(left, b[:, cols(f, FB)])
            total = t if total is None else total + t
            back = q if back is None else back + q
        return total, back

    def step_m(k):
        kk = k // parts
        active = mine(k)
        wait(g.at[k, 0, pl.ds(0, Y - 1)], r_y.at[k])
        send(g.at[k, core], g.at[k, core], s_c.at[k], r_c.at[k], dev(dp=d + 1 - 2 * core))
        total, back = half(k, core)
        pacc[...] = total
        bacc[...] = back
        wait(g.at[k, 0], r_c.at[k])
        total, back = half(k, 1 - core)
        back = bacc[...] + back
        bacc[...] = back

        @pl.when(active)
        def _():
            bx[x, kk] = bacc[rows(y * OWNERS + place, T), :]
            for j in range(1, X):
                send(bx.at[x, kk], bx.at[x, kk], s_b.at[kk], r_one.at[5], dev(tensor=(x + j) % X))

        first = (k % parts) * OWNERS
        spread = se[:, pl.ds(first, OWNERS), rows(kk, T), :].reshape(Y * OWNERS * T, R)
        weighted = (back * spread).astype(BF)
        pacc[...] += total + dot_nt(weighted, ai[...])

        @pl.when(same)
        def _():
            pacc[...] += g[k, core, :, zh].reshape(Y * OWNERS * T, FB).astype(F32)

        pb[k] = pacc[...].astype(BF).reshape(Y, OWNERS, T, FB)
        for j in range(1, X):
            r = (x + j) % X
            send(pb.at[k, r], rx.at[k, x], s_x.at[k], r_x.at[k], dev(tensor=r))
        own[k] = pacc[rows(x, OWNERS * T), :]

        @pl.when(jnp.logical_and(active, sec < S - 1))
        def _():
            for c in range(2):
                for zz in range(2):
                    send(g.at[k, c, y, zz, place], out.at[kk, c, zz], s_o.at[kk], r_one.at[4], dev(section=sec + 1))

    def step_x(k):
        kk = k // parts
        wait(rx.at[k, pl.ds(0, X - 1)], r_x.at[k])
        total = own[k]
        for j in range(1, X):
            total = total + rx[k, (x + j) % X].reshape(OWNERS * T, FB).astype(F32)
        sp[k] = total.astype(BF).reshape(OWNERS, T, FB)

        @pl.when(sec > 0)
        def _():
            send(sp.at[k], g.at[k, core, x, zh], s_p.at[k], r_s.at[k],
                 dev(dp=x * SUBS + m, section=sec - 1, tensor=y))

        @pl.when(bottom)
        def _():
            for o in range(OWNERS):
                owner = (k % parts) * OWNERS + o
                here = jnp.logical_and(same, m == owner)

                @pl.when(here)
                def _():
                    pltpu.make_async_copy(sp.at[k, o], out.at[kk, core, zh], r_one.at[4]).start()

                @pl.when(jnp.logical_not(here))
                def _():
                    send(sp.at[k, o], out.at[kk, core, zh], s_p.at[k], r_one.at[4],
                         dev(dp=x * SUBS + owner, tensor=y))

    NK = N // parts
    tokens = NK * T
    FD = hl.shape[2]

    def scalings():
        wait(bx.at[pl.ds(0, X - 1)], r_one.at[5])
        wait(dx.at[pl.ds(0, X - 1)], r_one.at[3])
        back = bx[0].reshape(tokens, R)
        down = dx[0]
        for j in range(1, X):
            back = back + bx[j].reshape(tokens, R)
            down = down + dx[j]
        product = down * back
        expert = lax.broadcasted_iota(jnp.int32, (ex, R), 0)
        column = lax.broadcasted_iota(jnp.int32, (ex, R), 1)
        group = jnp.where(expert == lax.div(column, rank), 1.0, 0.0).astype(F32)
        turned = dot_nt(group, product, lax.Precision.HIGHEST)
        sga[sec] = turned
        for j in range(1, S):
            send(sga.at[sec], sga.at[sec], s_one.at[5], r_one.at[6], dev(section=(sec + j) % S))
        per = tokens // mix.shape[0]
        for i in range(mix.shape[0]):
            scale[i] = turned[:, i * per:(i + 1) * per]

        wait(states, l_one.at[5])
        t_hi = turned.astype(BF)
        t_lo = (turned - t_hi.astype(F32)).astype(BF)
        sums = (jnp.dot(t_hi, states[...], preferred_element_type=F32)
                + jnp.dot(t_lo, states[...], preferred_element_type=F32))
        for e in range(DP):
            hl[e] = sums[:, e * FD:(e + 1) * FD]
        for j in range(1, DP):
            e = (d + j) % DP
            send(hl.at[e], hx.at[d], s_one.at[6], r_one.at[7], dev(dp=e))
        hx[d] = hl[d]

    steps = {"S": step_s, "Z": step_z, "M": step_m, "X": step_x}
    behind = dict(ORDER)

    turns = N + max(behind.values())

    @pl.loop(0, turns + 1)
    def _(i):
        @pl.when(i == jnp.where(top, behind["M"], 0))
        def _():
            prepare()

        @pl.when(i == jnp.where(bottom, N + behind["M"], turns))
        def _():
            scalings()

        for name, lag in ORDER:
            @pl.when(jnp.logical_and(i >= lag, i < N + lag))
            def _():
                steps[name](i - lag)

    wait(hx.at[pl.ds(0, DP - 1)], r_one.at[7])
    total = hx[0]
    for j in range(1, DP):
        total = total + hx[j]
    total = total * (1.0 / math.sqrt(tokens * DP))
    hg[d] = total
    for j in range(1, DP):
        send(hg.at[d], hg.at[d], s_one.at[7], r_one.at[8], dev(dp=(d + j) % DP))

    wait(cta, r_one.at[2])
    wait(sga.at[pl.ds(0, S - 1)], r_one.at[6])
    left = sga[...].reshape(S * ex, tokens).T
    right = cta[...].reshape(S * ex, -1)
    hidden[...] = jnp.dot(left, right, precision=lax.Precision.HIGHEST, preferred_element_type=F32)

    wait(hx.at[pl.ds(0, DP - 1)], r_one.at[8])
    for e in range(DP):
        head[:, e * FD:(e + 1) * FD] = hg[e]
    wait(out, r_one.at[4])
    wait(sall.at[pl.ds(0, DP - 1)], s_one.at[0])

    @pl.when(apart)
    def _():
        wait(ai, s_one.at[1])

    wait(cta.at[pl.ds(0, S - 1)], s_one.at[2])
    wait(dx.at[pl.ds(0, X - 1)], s_one.at[3])
    wait(sga.at[pl.ds(0, S - 1)], s_one.at[5])
    wait(hx.at[pl.ds(0, DP - 1)], s_one.at[6])
    wait(hx.at[pl.ds(0, DP - 1)], s_one.at[7])

    @pl.loop(0, N)
    def _(k):
        kk = k // parts
        wait(g.at[k, 0, :, 0], s_s.at[k])
        wait(g.at[k, 0, pl.ds(0, Y - 1), 0], s_z.at[k])
        wait(g.at[k, 0], s_c.at[k])
        wait(rx.at[k, pl.ds(0, X - 1)], s_x.at[k])
        active = mine(k)

        @pl.when(active)
        def _():
            wait(bx.at[pl.ds(0, X - 1), kk], s_b.at[kk])

            @pl.when(top)
            def _():
                wait(out.at[kk, 0, pl.ds(0, 1)], s_u.at[k])
                wait(out.at[kk, 1], s_u.at[k])

            @pl.when(sec < S - 1)
            def _():
                wait(out.at[kk], s_o.at[kk])

        local = jnp.logical_and(jnp.logical_and(bottom, same), active)

        @pl.when(local)
        def _():
            if OWNERS > 1:
                wait(sp.at[k, pl.ds(0, OWNERS - 1)], s_p.at[k])

        @pl.when(jnp.logical_not(local))
        def _():
            wait(sp.at[k], s_p.at[k])


def on_device(u, saved, w, a, b, mix, states, classifier):
    X, S, DP = (lax.axis_size(n) for n in ("tensor", "section", "dp"))
    Y = DP // SUBS
    micro, per, F = u.shape
    T = TOK
    tokens = micro * per
    NK = tokens // T
    N = NK * (SUBS // OWNERS)
    FB = w.shape[2]
    R = a.shape[2]
    ex = mix.shape[2]
    vmem = pl.BlockSpec(memory_space=pltpu.VMEM)
    far = pl.BlockSpec(memory_space=pltpu.HBM)
    dma = pltpu.SemaphoreType.DMA
    sizes = (X, Y, S, DP, N, R)
    out, scale, head, hidden = pl.pallas_call(
        functools.partial(kernel, sizes),
        out_shape=(
            jax.ShapeDtypeStruct((NK, 2, 2, T, FB), BF),
            jax.ShapeDtypeStruct((micro, ex, per), F32),
            jax.ShapeDtypeStruct((ex, F), F32),
            jax.ShapeDtypeStruct((tokens, F), F32),
        ),
        in_specs=[far] * 8,
        out_specs=(vmem,) * 4,
        scratch_shapes=[
            pltpu.VMEM((NK, T, F), BF),
            pltpu.VMEM((NK, SUBS, T, FB), BF),
            pltpu.VMEM((tokens, F), BF),
            pltpu.VMEM((F, FB), BF),
            pltpu.VMEM((F, R), BF),
            pltpu.VMEM((R, F), BF),
            pltpu.VMEM((micro, ex, per), F32),
            pltpu.VMEM((tokens, F), BF),
            pltpu.VMEM((N, 2, Y, 2, OWNERS, T, FB), BF),
            pltpu.VMEM((N, Y, OWNERS, T, FB), BF),
            pltpu.VMEM((N, X, OWNERS, T, FB), BF),
            pltpu.VMEM((N, OWNERS * T, FB), F32),
            pltpu.VMEM((N, OWNERS, T, FB), BF),
            pltpu.VMEM((Y, SUBS, tokens, R), F32),
            pltpu.VMEM((2 * ex, tokens), BF),
            pltpu.VMEM((DP, 2 * ex, tokens), BF),
            pltpu.VMEM((FB, R), BF),
            pltpu.VMEM((X, tokens, R), F32),
            pltpu.VMEM((X, NK, T, R), F32),
            pltpu.VMEM((Y * OWNERS * T, FB), F32),
            pltpu.VMEM((Y * OWNERS * T, R), F32),
            pltpu.VMEM((S, ex, F), F32),
            pltpu.VMEM((S, ex, tokens), F32),
            pltpu.VMEM((DP, ex, F // DP), F32),
            pltpu.VMEM((DP, ex, F // DP), F32),
            pltpu.VMEM((DP, ex, F // DP), F32),
        ] + [dma((N,))] * 13 + [dma((9,)), dma((8,)), dma((7,))],
        compiler_params=pltpu.CompilerParams(
            collective_id=0, has_side_effects=True, vmem_limit_bytes=60 * 1024 * 1024,
        ),
    )(
        u.reshape(NK, T, F),
        saved.reshape(tokens, F),
        w[0], a[0], b[0],
        mix.transpose(0, 2, 1),
        states.reshape(tokens, F),
        classifier.T,
    )
    grads = out.reshape(micro, per // T, 2, 2, T, FB).transpose(0, 1, 4, 3, 2, 5).reshape(1, micro, per, F)
    return grads, scale.transpose(0, 2, 1), head.T, hidden.reshape(micro, per, F)


def solution(mesh):
    return jax.shard_map(
        on_device,
        mesh=mesh,
        in_specs=(
            P(None, "dp", "tensor"),
            P("section", None, "dp", "tensor"),
            P("section", "tensor", "dp"),
            P("section", "tensor", None),
            P("section", None, "tensor"),
            P(None, "dp", "section"),
            P(None, "dp", "tensor"),
            P("tensor", "section"),
        ),
        out_specs=(
            P("section", None, "dp", "tensor"),
            P(None, "dp", "section"),
            P("tensor", "section"),
            P(None, "dp", "tensor"),
        ),
        check_vma=False,
    )
```

time: 249 us -> 213 us (0.86)
  Pallas kernels: 237 us -> 207 us
  local copies, waits for them, and re-layouts: 11.4 us -> 5.11 us
    pallas_call x1, Pallas kernels: 237 us -> 207 us  [on_device(): pl.pallas_call(functools.partial(kernel, sizes), out_shape=(jax.ShapeDtyp...]
    unnamed x16 -> x9, local copies, waits for them, and re-layouts: 9.57 us -> 2.25 us
where the time goes in v2:
time: 213 us; the launch traced here: 212 us
  Pallas kernels  207 us (97%)
  local copies, waits for them, and re-layouts  5.11 us (2%)
    pallas_call x1, Pallas kernels, on_device(): pl.pallas_call(functools.partial(kernel, sizes), out_shape=(jax.ShapeDtyp...  207 us

profile of v2, /device:TPU:1, one launch (start us, length us, event | category | flops | bytes accessed | tf_op | source)
XLA Modules:
  0.0 212.5 jit_solution(15633801682665794565)
XLA Ops:
  0.6 206.7 %shard_map.111 = (bf16[8,2,2,16,512]{4,3,2,1,0:T(8,128)(2,1)}, f32[4,16,32]{2,1,0:T(8,128)}, f32[16,2048]{1,0:T(8,128)}, f32[128,2048]{1,0:T(8,128)}) custom-call(bf16[8,16,2048]{2,1,0:T(8,128)(2,1)} %bitcast.18, bf16[128,2048]{1,0:T(8,128)(2,1)} %bitcast.19, bf16[2048,512]{1,0:T(8,128)(2,1)} %bitcast.14, bf16[2048,256]{1,0:T(8,128)(2,1)} %bitcast.16, ...), custom_call_target="tpu_custom_call" | custom-call | tf_op jit(solution)/shard_map/pallas_call | solution.py:402
  207.3 0.0 copy-start.2
  207.3 0.0 copy-start.1
  207.3 0.0 copy-start
  207.3 1.7 copy.12
  209.0 1.2 reshape.30
  210.2 0.0 copy-done.2
  210.2 0.6 copy.16
  210.8 0.0 copy-done.1
  210.8 0.7 copy.17
  211.5 0.0 copy-done
  211.5 1.0 copy.18
Async XLA Ops:
  207.3 2.9 %copy-start.2 = (f32[4,16,32]{2,1,0:T(8,128)S(1)}, f32[4,16,32]{2,1,0:T(8,128)}, u32[]{:S(2)}) copy-start(f32[4,16,32]{2,1,0:T(8,128)} %get-tuple-element.9) | copy-start | bytes 24580
  207.3 3.5 %copy-start.1 = (f32[16,2048]{1,0:T(8,128)S(1)}, f32[16,2048]{1,0:T(8,128)}, u32[]{:S(2)}) copy-start(f32[16,2048]{1,0:T(8,128)} %get-tuple-element.10) | copy-start | bytes 393220
  207.3 4.2 %copy-start = (f32[128,2048]{1,0:T(8,128)S(1)}, f32[128,2048]{1,0:T(8,128)}, u32[]{:S(2)}) copy-start(f32[128,2048]{1,0:T(8,128)} %get-tuple-element.11) | copy-start | bytes 3145732

commit v3 on v2

--- a/solution.py
+++ b/solution.py
@@ -14,7 +14,7 @@
 SUBS = 4
 TOK = 16
 OWNERS = 2
-ORDER = (("S", 0), ("M", 3), ("Z", 1), ("X", 4))
+ORDER = (("S", 0), ("M", 3), ("R", 1), ("Z", 1), ("X", 4))
 
 
 def dot_nt(a, b, precision=None):
@@ -24,11 +24,11 @@
 def kernel(
     sizes,
     u, hid_in, w_in, a_in, b_in, mix_in, states_in, ct,
-    out, scale, head, hidden,
-    uv, us, hid, w, a, b, mix, states,
+    grads, scale, head, hidden,
+    out, uv, us, hid, w, a, b, mix, states,
     g, pb, rx, own, sp, se, sb, sall, ai, dx, bx, pacc, bacc, cta, sga, hl, hx, hg,
-    r_s, r_z, r_y, r_c, r_x,
-    s_s, s_z, s_c, s_x, s_p, s_o, s_b, s_u,
+    r_s, r_z, r_y, r_c, r_x, r_p, r_n,
+    s_s, s_z, s_c, s_x, s_p, s_o, s_b, s_u, s_r,
     r_one, s_one, l_one,
 ):
     X, Y, S, DP, N, R = sizes
@@ -153,8 +153,19 @@
         block = g.at[k, core, y, zh]
         wait(block, r_s.at[k])
         send(block, block, s_s.at[k], r_z.at[k], dev(dp=(d + 2) % SUBS + y * SUBS))
-        for j in range(1, Y):
-            send(block, block, s_s.at[k], r_y.at[k], dev(dp=((y + j) % Y) * SUBS + m))
+        send(block, block, s_s.at[k], r_p.at[k], dev(dp=((y + 1) % Y) * SUBS + m))
+        send(block, block, s_s.at[k], r_n.at[k], dev(dp=((y + Y - 1) % Y) * SUBS + m))
+
+    def step_r(k):
+        before = (y + Y - 1) % Y
+        after = (y + 1) % Y
+        half = OWNERS // 2
+        wait(g.at[k, core, before, zh], r_p.at[k])
+        lower = g.at[k, core, before, zh, pl.ds(0, half)]
+        send(lower, lower, s_r.at[k], r_y.at[k], dev(dp=after * SUBS + m))
+        wait(g.at[k, core, after, zh], r_n.at[k])
+        upper = g.at[k, core, after, zh, pl.ds(half, half)]
+        send(upper, upper, s_r.at[k], r_y.at[k], dev(dp=before * SUBS + m))
 
     def step_z(k):
         block = g.at[k, core, y, 1 - zh]
@@ -198,7 +209,7 @@
     def step_m(k):
         kk = k // parts
         active = mine(k)
-        wait(g.at[k, 0, pl.ds(0, Y - 1)], r_y.at[k])
+        wait(g.at[k, 0, pl.ds(0, 2)], r_y.at[k])
         send(g.at[k, core], g.at[k, core], s_c.at[k], r_c.at[k], dev(dp=d + 1 - 2 * core))
         total, back = half(k, core)
         pacc[...] = total
@@ -293,13 +304,13 @@
         sums = (jnp.dot(t_hi, states[...], preferred_element_type=F32)
                 + jnp.dot(t_lo, states[...], preferred_element_type=F32))
         for e in range(DP):
-            hl[e] = sums[:, e * FD:(e + 1) * FD]
+            hl[e] = sums[:, e * FD:(e + 1) * FD].astype(BF)
         for j in range(1, DP):
             e = (d + j) % DP
             send(hl.at[e], hx.at[d], s_one.at[6], r_one.at[7], dev(dp=e))
         hx[d] = hl[d]
 
-    steps = {"S": step_s, "Z": step_z, "M": step_m, "X": step_x}
+    steps = {"S": step_s, "Z": step_z, "R": step_r, "M": step_m, "X": step_x}
     behind = dict(ORDER)
 
     turns = N + max(behind.values())
@@ -320,11 +331,10 @@
                 steps[name](i - lag)
 
     wait(hx.at[pl.ds(0, DP - 1)], r_one.at[7])
-    total = hx[0]
+    total = hx[0].astype(F32)
     for j in range(1, DP):
-        total = total + hx[j]
-    total = total * (1.0 / math.sqrt(tokens * DP))
-    hg[d] = total
+        total = total + hx[j].astype(F32)
+    hg[d] = (total * (1.0 / math.sqrt(tokens * DP))).astype(BF)
     for j in range(1, DP):
         send(hg.at[d], hg.at[d], s_one.at[7], r_one.at[8], dev(dp=(d + j) % DP))
 
@@ -336,8 +346,10 @@
 
     wait(hx.at[pl.ds(0, DP - 1)], r_one.at[8])
     for e in range(DP):
-        head[:, e * FD:(e + 1) * FD] = hg[e]
+        head[:, e * FD:(e + 1) * FD] = hg[e].astype(F32)
     wait(out, r_one.at[4])
+    for f in range(SUBS):
+        grads[:, :, f * FB:(f + 1) * FB] = out[:, f % 2, f // 2]
     wait(sall.at[pl.ds(0, DP - 1)], s_one.at[0])
 
     @pl.when(apart)
@@ -353,7 +365,8 @@
     @pl.loop(0, N)
     def _(k):
         kk = k // parts
-        wait(g.at[k, 0, :, 0], s_s.at[k])
+        wait(g.at[k, 0, pl.ds(0, Y - 1), 0], s_s.at[k])
+        wait(g.at[k, 0, 0, 0], s_r.at[k])
         wait(g.at[k, 0, pl.ds(0, Y - 1), 0], s_z.at[k])
         wait(g.at[k, 0], s_c.at[k])
         wait(rx.at[k, pl.ds(0, X - 1)], s_x.at[k])
@@ -382,6 +395,14 @@
         @pl.when(jnp.logical_not(local))
         def _():
             wait(sp.at[k], s_p.at[k])
+
+
+def finish(*refs):
+    copies = [pltpu.make_async_copy(refs[i], refs[4 + i], refs[8].at[i]) for i in range(4)]
+    for copy in copies:
+        copy.start()
+    for copy in copies:
+        copy.wait()
 
 
 def on_device(u, saved, w, a, b, mix, states, classifier):
@@ -399,17 +420,19 @@
     far = pl.BlockSpec(memory_space=pltpu.HBM)
     dma = pltpu.SemaphoreType.DMA
     sizes = (X, Y, S, DP, N, R)
-    out, scale, head, hidden = pl.pallas_call(
+    shapes = (
+        jax.ShapeDtypeStruct((NK, T, F), BF),
+        jax.ShapeDtypeStruct((micro, ex, per), F32),
+        jax.ShapeDtypeStruct((ex, F), F32),
+        jax.ShapeDtypeStruct((tokens, F), F32),
+    )
+    results = pl.pallas_call(
         functools.partial(kernel, sizes),
-        out_shape=(
-            jax.ShapeDtypeStruct((NK, 2, 2, T, FB), BF),
-            jax.ShapeDtypeStruct((micro, ex, per), F32),
-            jax.ShapeDtypeStruct((ex, F), F32),
-            jax.ShapeDtypeStruct((tokens, F), F32),
-        ),
+        out_shape=shapes,
         in_specs=[far] * 8,
         out_specs=(vmem,) * 4,
         scratch_shapes=[
+            pltpu.VMEM((NK, 2, 2, T, FB), BF),
             pltpu.VMEM((NK, T, F), BF),
             pltpu.VMEM((NK, SUBS, T, FB), BF),
             pltpu.VMEM((tokens, F), BF),
@@ -433,10 +456,10 @@
             pltpu.VMEM((Y * OWNERS * T, R), F32),
             pltpu.VMEM((S, ex, F), F32),
             pltpu.VMEM((S, ex, tokens), F32),
-            pltpu.VMEM((DP, ex, F // DP), F32),
-            pltpu.VMEM((DP, ex, F // DP), F32),
-            pltpu.VMEM((DP, ex, F // DP), F32),
-        ] + [dma((N,))] * 13 + [dma((9,)), dma((8,)), dma((7,))],
+            pltpu.VMEM((DP, ex, F // DP), BF),
+            pltpu.VMEM((DP, ex, F // DP), BF),
+            pltpu.VMEM((DP, ex, F // DP), BF),
+        ] + [dma((N,))] * 16 + [dma((9,)), dma((8,)), dma((7,))],
         compiler_params=pltpu.CompilerParams(
             collective_id=0, has_side_effects=True, vmem_limit_bytes=60 * 1024 * 1024,
         ),
@@ -448,7 +471,14 @@
         states.reshape(tokens, F),
         classifier.T,
     )
-    grads = out.reshape(micro, per // T, 2, 2, T, FB).transpose(0, 1, 4, 3, 2, 5).reshape(1, micro, per, F)
+    grads, scale, head, hidden = pl.pallas_call(
+        finish,
+        out_shape=shapes,
+        in_specs=[vmem] * 4,
+        out_specs=(far,) * 4,
+        scratch_shapes=[dma((4,))],
+    )(*results)
+    grads = grads.reshape(1, micro, per, F)
     return grads, scale.transpose(0, 2, 1), head.T, hidden.reshape(micro, per, F)
 
 

time: 213 us -> 204 us (0.958)
  local copies, waits for them, and re-layouts: 5.11 us -> 0 us
  Pallas kernels: 207 us -> 203 us
    pallas_call x1 -> x2, Pallas kernels: 207 us -> 203 us  [the longest x1 200 us: on_device(): pl.pallas_call(functools.partial(kernel, sizes), out_shape=shapes, in_spe...]
    unnamed x9 -> x0, local copies, waits for them, and re-layouts: 2.25 us -> none
where the time goes in v3:
time: 204 us
  Pallas kernels  203 us (100%)
    pallas_call x1, Pallas kernels, on_device(): pl.pallas_call(functools.partial(kernel, sizes), out_shape=shapes, in_spe...  200 us

profile of v3, /device:TPU:1, one launch (start us, length us, event | category | flops | bytes accessed | tf_op | source)
XLA Modules:
  0.0 203.7 jit_solution(15795373692225237021)
XLA Ops:
  0.6 200.4 %shard_map.111 = (bf16[8,16,2048]{2,1,0:T(8,128)(2,1)}, f32[4,16,32]{2,1,0:T(8,128)}, f32[16,2048]{1,0:T(8,128)}, f32[128,2048]{1,0:T(8,128)}) custom-call(bf16[8,16,2048]{2,1,0:T(8,128)(2,1)} %bitcast.15, bf16[128,2048]{1,0:T(8,128)(2,1)} %bitcast.16, bf16[2048,512]{1,0:T(8,128)(2,1)} %bitcast.12, bf16[2048,256]{1,0:T(8,128)(2,1)} %bitcast.13, ...), custom_call_target="tpu_custom_call" | custom-call | tf_op jit(solution)/shard_map/pallas_call | solution.py:429
  201.0 2.7 %shard_map.112 = (bf16[8,16,2048]{2,1,0:T(8,128)(2,1)}, f32[4,16,32]{2,1,0:T(8,128)}, f32[16,2048]{1,0:T(8,128)}, f32[128,2048]{1,0:T(8,128)}) custom-call(bf16[8,16,2048]{2,1,0:T(8,128)(2,1)} %get-tuple-element.12.refs_0_, f32[4,16,32]{2,1,0:T(8,128)} %get-tuple-element.13.refs_1_, f32[16,2048]{1,0:T(8,128)} %get-tuple-element.14.refs_2_, ...), custom_call_target="tpu_custom_call" | custom-call | tf_op jit(solution)/shard_map/pallas_call | solution.py:474

commit v4 on v3

--- a/solution.py
+++ b/solution.py
@@ -170,7 +170,7 @@
     def step_z(k):
         block = g.at[k, core, y, 1 - zh]
         wait(block, r_z.at[k])
-        for j in range(1, Y):
+        for j in (2, 1, 3):
             send(block, block, s_z.at[k], r_y.at[k], dev(dp=((y + j) % Y) * SUBS + m))
 
     def prepare():

time: 204 us -> 202 us (level)
  no operation moved by 1% of the time
where the time goes in v4:
time: 202 us
  Pallas kernels  201 us (100%)
    pallas_call x1, Pallas kernels, on_device(): pl.pallas_call(functools.partial(kernel, sizes), out_shape=shapes, in_spe...  199 us

profile of v4, /device:TPU:1, one launch (start us, length us, event | category | flops | bytes accessed | tf_op | source)
XLA Modules:
  0.0 202.0 jit_solution(6840055342990323513)
XLA Ops:
  0.6 198.7 %shard_map.111 = (bf16[8,16,2048]{2,1,0:T(8,128)(2,1)}, f32[4,16,32]{2,1,0:T(8,128)}, f32[16,2048]{1,0:T(8,128)}, f32[128,2048]{1,0:T(8,128)}) custom-call(bf16[8,16,2048]{2,1,0:T(8,128)(2,1)} %bitcast.15, bf16[128,2048]{1,0:T(8,128)(2,1)} %bitcast.16, bf16[2048,512]{1,0:T(8,128)(2,1)} %bitcast.12, bf16[2048,256]{1,0:T(8,128)(2,1)} %bitcast.13, ...), custom_call_target="tpu_custom_call" | custom-call | tf_op jit(solution)/shard_map/pallas_call | solution.py:429
  199.3 2.7 %shard_map.112 = (bf16[8,16,2048]{2,1,0:T(8,128)(2,1)}, f32[4,16,32]{2,1,0:T(8,128)}, f32[16,2048]{1,0:T(8,128)}, f32[128,2048]{1,0:T(8,128)}) custom-call(bf16[8,16,2048]{2,1,0:T(8,128)(2,1)} %get-tuple-element.12.refs_0_, f32[4,16,32]{2,1,0:T(8,128)} %get-tuple-element.13.refs_1_, f32[16,2048]{1,0:T(8,128)} %get-tuple-element.14.refs_2_, ...), custom_call_target="tpu_custom_call" | custom-call | tf_op jit(solution)/shard_map/pallas_call | solution.py:474

commit v5 on v4

--- a/solution.py
+++ b/solution.py
@@ -344,12 +344,13 @@
     right = cta[...].reshape(S * ex, -1)
     hidden[...] = jnp.dot(left, right, precision=lax.Precision.HIGHEST, preferred_element_type=F32)
 
+    wait(out, r_one.at[4])
+    for f in range(SUBS):
+        grads[:, :, f * FB:(f + 1) * FB] = out[:, f % 2, f // 2]
+
     wait(hx.at[pl.ds(0, DP - 1)], r_one.at[8])
     for e in range(DP):
         head[:, e * FD:(e + 1) * FD] = hg[e].astype(F32)
-    wait(out, r_one.at[4])
-    for f in range(SUBS):
-        grads[:, :, f * FB:(f + 1) * FB] = out[:, f % 2, f // 2]
     wait(sall.at[pl.ds(0, DP - 1)], s_one.at[0])
 
     @pl.when(apart)

time: 202 us -> 202 us (level)
  no operation moved by 1% of the time
where the time goes in v5:
time: 202 us
  Pallas kernels  201 us (100%)
    pallas_call x1, Pallas kernels, on_device(): pl.pallas_call(functools.partial(kernel, sizes), out_shape=shapes, in_spe...  199 us

profile of v5, /device:TPU:1, one launch (start us, length us, event | category | flops | bytes accessed | tf_op | source)
XLA Modules:
  0.0 202.0 jit_solution(3970581904663762183)
XLA Ops:
  0.6 198.6 %shard_map.111 = (bf16[8,16,2048]{2,1,0:T(8,128)(2,1)}, f32[4,16,32]{2,1,0:T(8,128)}, f32[16,2048]{1,0:T(8,128)}, f32[128,2048]{1,0:T(8,128)}) custom-call(bf16[8,16,2048]{2,1,0:T(8,128)(2,1)} %bitcast.15, bf16[128,2048]{1,0:T(8,128)(2,1)} %bitcast.16, bf16[2048,512]{1,0:T(8,128)(2,1)} %bitcast.12, bf16[2048,256]{1,0:T(8,128)(2,1)} %bitcast.13, ...), custom_call_target="tpu_custom_call" | custom-call | tf_op jit(solution)/shard_map/pallas_call | solution.py:430
  199.3 2.7 %shard_map.112 = (bf16[8,16,2048]{2,1,0:T(8,128)(2,1)}, f32[4,16,32]{2,1,0:T(8,128)}, f32[16,2048]{1,0:T(8,128)}, f32[128,2048]{1,0:T(8,128)}) custom-call(bf16[8,16,2048]{2,1,0:T(8,128)(2,1)} %get-tuple-element.12.refs_0_, f32[4,16,32]{2,1,0:T(8,128)} %get-tuple-element.13.refs_1_, f32[16,2048]{1,0:T(8,128)} %get-tuple-element.14.refs_2_, ...), custom_call_target="tpu_custom_call" | custom-call | tf_op jit(solution)/shard_map/pallas_call | solution.py:475
